TPU v7x, 128 devices: a whole 4x4x4 slice. The times are simulated.
128 devices in a mesh: blk: 32 (over z, x, y_lo), grp: 4 (over y_hi, core).
Axes of the slice: x: 4, y: 4 (y_hi: 2, y_lo: 2; y = y_hi * 2 + y_lo), z: 4, core: 2. Of those that a mesh axis runs over, the one named last changes fastest.
Arguments:
- queries: bfloat16 [2048, 2048], P(('blk', 'grp')), may hold values from -0.125 to 0.125
- training: bfloat16 [131072, 2048], P(('blk', 'grp')), may hold values from -24 to 24
Outputs:
- scores: float32 [2048, 131072], P(None, ('blk', 'grp'))
- gram: float32 [2048, 2048], P(('blk', 'grp'))
All inputs are finite; a program needn't handle non-finite values.
Results may differ from a plain program's by a relative error of at most 0.0003.
Values may be sent and summed in bfloat16 or wider, within the bound.
A program may use at most 128 MiB of HBM per device.

v0:
```python
import jax
import jax.numpy as jnp
from jax import lax
from jax.sharding import PartitionSpec as P


def local(queries, training):
    scores = lax.dot_general(
        lax.all_gather(queries, ("blk", "grp"), axis=0, tiled=True),
        training,
        (((1,), (1,)), ((), ())),
        preferred_element_type=jnp.float32,
    )
    n_blk = lax.axis_size("blk")
    n_grp = lax.axis_size("grp")
    inverse = 1.0 / (training.shape[0] * n_blk * n_grp)
    partial_gram = (
        lax.dot_general(
            training, training, (((0,), (0,)), ((), ())), preferred_element_type=jnp.float32
        )
        * inverse
    )
    gram = lax.psum_scatter(partial_gram, ("blk", "grp"), scatter_dimension=0, tiled=True)
    return (scores, gram)


def solution(mesh):
    in_specs = (P(("blk", "grp"), None), P(("blk", "grp"), None))
    out_specs = (P(None, ("blk", "grp")), P(("blk", "grp"), None))
    return jax.shard_map(local, mesh=mesh, in_specs=in_specs, out_specs=out_specs, check_vma=False)
```

profile of v0, /device:TPU:1, one launch (start us, length us, event | category | flops | bytes accessed | tf_op | source)
XLA Modules:
  0.0 886.8 jit_solution(11934253866635188691)
XLA Ops:
  7.2 0.0 all-gather.2.cloned.1.call-start
  7.2 0.7 all-gather.2.cloned.1.call-update
  7.9 0.0 reduce-scatter.2.cloned.1.call-start
  7.9 15.2 %convolution_multiply_fusion = f32[2048,2048]{1,0:T(8,128)} fusion(bf16[1024,2048]{1,0:T(8,128)(2,1)} %param.3), kind=kOutput, calls=%fused_computation | convolution fusion | flops 8594128896 | bytes 20971520 | tf_op jit(solution)/shard_map/dot_general | solution.py:18
  23.1 0.0 reduce-scatter.2.cloned.1.call-update
  23.2 192.7 %all-gather.2.cloned.1.call-done = bf16[2048,2048]{1,0:T(8,128)(2,1)} async-done(((bf16[16,2048]{1,0:T(8,128)(2,1)}), bf16[2048,2048]{1,0:T(8,128)(2,1)}) %all-gather.2.cloned.1.call-update) | async-done | bytes 8388624 | tf_op jit(solution)/shard_map/all_gather | solution.py:9
  215.9 14.5 %fusion = f32[2048,1024]{1,0:T(8,128)} fusion(bf16[2048,2048]{1,0:T(8,128)(2,1)} %all-gather.2.cloned.1.call-done, bf16[1024,2048]{1,0:T(8,128)(2,1)} %param.3), kind=kOutput, calls=%fused_computation.1 | convolution fusion | flops 8589934592 | bytes 20971520 | tf_op jit(solution)/shard_map/dot_general | solution.py:8
  230.5 649.5 %reduce-scatter.2.cloned.1.call-done = f32[16,2048]{1,0:T(8,128)} async-done(((f32[2048,2048]{1,0:T(8,128)}), f32[16,2048]{1,0:T(8,128)}) %reduce-scatter.2.cloned.1.call-update) | async-done | bytes 131088 | tf_op jit(solution)/shard_map/reduce_scatter | solution.py:23
Async XLA Ops:
  7.2 208.8 %all-gather.2.cloned.1.call-start = ((), (), s32[]{:S(2)}) async-start(), calls=%async_computation.1 | async-start | bytes 8454144 | tf_op jit(solution)/shard_map/all_gather | solution.py:9
  7.9 872.1 %reduce-scatter.2.cloned.1.call-start = ((), (), s32[]{:S(2)}) async-start(), calls=%async_computation.2 | async-start | bytes 16908288 | tf_op jit(solution)/shard_map/reduce_scatter | solution.py:23
Sparse Core Ops, SparseCore 0:
  9.7 206.1 all-gather.1
  218.9 661.0 reduce-scatter.1
where the time goes:
time: 893 us; the launch traced here: 887 us
  waiting for transfers between devices  843 us (94%)
  matrix products  29.7 us (3%)
  between operations  14 us (2%)
    reduce_scatter x1, waiting for transfers between devices, local(): lax.psum_scatter(partial_gram, ('blk', 'grp'), scatter_dimension=0, tiled...  650 us
    all_gather x1, waiting for transfers between devices, local(): lax.all_gather(queries, ('blk', 'grp'), axis=0, tiled=True)  193 us
  transfers between devices with their start and end apart: 2, of which 2 were waited for; matrix products, arithmetic and copies ran while one was open for 3% of the time, Pallas kernels for 0%

commit v1 on v0

v1 whole, which is shorter than its diff:
```python
import functools

import jax
import jax.numpy as jnp
from jax import lax
from jax.experimental import pallas as pl
from jax.experimental.pallas import tpu as pltpu
from jax.sharding import PartitionSpec as P

MESH = pl.DeviceIdType.MESH
ALL = pl.ds(0, 4)
AXES = ("z", "x", "y")
B = 128
CH = 136
AG_PARTS = (((0, 640), "yxz"), ((640, 1280), "zyx"), ((1280, 2048), "xzy"))
RS_PARTS = (((0, 48), "zxy"), ((48, 96), "xyz"), ((96, 136), "yzx"))
N_SEM = 160


def stored(axis, i):
    return lax.rem(i, 2) * 2 + lax.div(i, 2) if axis == "y" else i


class Net:
    def __init__(self, ssem, rsem):
        blk, grp = lax.axis_index("blk"), lax.axis_index("grp")
        self.at = {
            "z": lax.div(blk, 8),
            "x": lax.rem(lax.div(blk, 2), 4),
            "y": lax.div(grp, 2) * 2 + lax.rem(blk, 2),
        }
        self.core = lax.rem(grp, 2)
        self.group = lax.div(blk, 2)
        self.k = lax.rem(blk, 2) * 4 + grp
        self.ssem, self.rsem = ssem, rsem
        self.count = 0
        self.sent = []

    def device(self, core=None, **moved):
        at = {**self.at, **moved}
        core = self.core if core is None else core
        return (at["z"] * 8 + at["x"] * 2 + lax.rem(at["y"], 2), lax.div(at["y"], 2) * 2 + core)

    def hop(self, axis, by):
        return lax.rem(self.at[axis] + by + 4, 4)

    def neighbour(self, axis, by):
        return self.device(**{axis: self.hop(axis, by)})

    def sibling(self):
        return self.device(core=1 - self.core)

    def send(self, src, dst, to):
        t = self.count
        self.count += 1
        copy = pltpu.make_async_remote_copy(
            src_ref=src,
            dst_ref=dst,
            send_sem=self.ssem.at[t],
            recv_sem=self.rsem.at[t],
            device_id=to,
            device_id_type=MESH,
        )
        copy.start()
        self.sent.append(copy)
        return copy


def member(group, k):
    return (group * 2 + lax.div(k, 4), lax.rem(k, 4))


def gather_part(net, q, cols, order):
    lo, hi = cols

    def region(idx, c=None):
        at = [idx[a] for a in AXES]
        return q.at[at[0], at[1], at[2], net.core, :, pl.ds(lo, hi - lo)] if c is None else q.at[
            at[0], at[1], at[2], net.core, :, pl.ds(*c)
        ]

    def halves(idx):
        free = [a for a in AXES if isinstance(idx[a], pl.Slice)]
        if free:
            return [region({**idx, free[0]: pl.ds(2 * h, 2)}) for h in range(2)]
        mid = (hi - lo) // 256 * 128
        return [region(idx, (lo, mid)), region(idx, (lo + mid, hi - lo - mid))]

    idx = {a: stored(a, net.at[a]) for a in AXES}
    to_sibling = []
    to_sibling.append(net.send(region(idx), region(idx), net.sibling()))
    for axis in order:
        here = region(idx)
        up = net.send(here, here, net.neighbour(axis, 1))
        down = net.send(here, here, net.neighbour(axis, -1))
        from_low = {**idx, axis: stored(axis, net.hop(axis, -1))}
        from_high = {**idx, axis: stored(axis, net.hop(axis, 1))}
        far = {**idx, axis: stored(axis, net.hop(axis, 2))}
        yield
        up.wait_recv()
        src = halves(from_low)[0]
        on_up = net.send(src, src, net.neighbour(axis, 1))
        to_sibling.append(net.send(region(from_low), region(from_low), net.sibling()))
        down.wait_recv()
        src = halves(from_high)[1]
        on_down = net.send(src, src, net.neighbour(axis, -1))
        to_sibling.append(net.send(region(from_high), region(from_high), net.sibling()))
        yield
        on_up.wait_recv()
        on_down.wait_recv()
        to_sibling.append(net.send(region(far), region(far), net.sibling()))
        idx = {**idx, axis: ALL}
    yield
    for copy in to_sibling:
        copy.wait_recv()


def reduce_part(net, p, bufs, rows, order):
    lo, hi = rows

    def region(idx, r=None):
        at = [idx[a] for a in AXES]
        r = (lo, hi - lo) if r is None else r
        return p.at[at[0], at[1], at[2], net.core, pl.ds(*r)]

    def halves(idx):
        free = [a for a in AXES if isinstance(idx[a], pl.Slice)]
        if free:
            return [region({**idx, free[0]: pl.ds(2 * h, 2)}) for h in range(2)]
        mid = (hi - lo + 8) // 16 * 8
        return [region(idx, (lo, mid)), region(idx, (lo + mid, hi - lo - mid))]

    idx = {a: ALL for a in AXES}
    for axis, buf in zip(order, bufs, strict=True):
        far = halves({**idx, axis: stored(axis, net.hop(axis, 2))})
        high = halves({**idx, axis: stored(axis, net.hop(axis, 1))})
        low = halves({**idx, axis: stored(axis, net.hop(axis, -1))})
        idx = {**idx, axis: stored(axis, net.at[axis])}
        mine = halves(idx)
        up, down = net.neighbour(axis, 1), net.neighbour(axis, -1)
        via_up = net.send(far[0], buf[0], up)
        via_down = net.send(far[1], buf[1], down)
        own_up = net.send(high[1], buf[2], up)
        own_down = net.send(low[0], buf[3], down)
        yield
        via_up.wait_recv()
        high[0][...] += buf[0][...]
        sum_up = net.send(high[0], buf[4], up)
        via_down.wait_recv()
        low[1][...] += buf[1][...]
        sum_down = net.send(low[1], buf[5], down)
        yield
        own_up.wait_recv()
        sum_down.wait_recv()
        mine[1][...] += buf[2][...] + buf[5][...]
        own_down.wait_recv()
        sum_up.wait_recv()
        mine[0][...] += buf[3][...] + buf[4][...]


def part_buffers(rows):
    lo, hi = rows
    n = hi - lo
    mid = (n + 8) // 16 * 8
    shapes = []
    for lead in ((2, 4), (2,)):
        shapes.append([lead + (n, B)] * 6)
    shapes.append([(h, B) for h in (mid, n - mid, n - mid, mid, mid, n - mid)])
    return shapes


def step_all(gens):
    left = False
    for g in list(gens):
        try:
            next(g)
            left = True
        except StopIteration:
            gens.remove(g)
    return left


def kernel(scale, *refs):
    (q_in, t_in, s_out, g_out, q, t, p, d2d, s, x, slots) = refs[:11]
    n_rs = 18 * len(RS_PARTS)
    flat = refs[11 : 11 + n_rs]
    ssem, rsem, xsem, lsem = refs[11 + n_rs :]
    bufs = [
        [flat[18 * i + 6 * j : 18 * i + 6 * j + 6] for j in range(3)] for i in range(len(RS_PARTS))
    ]
    net = Net(ssem, rsem)
    zi, xi, yi = (stored(a, net.at[a]) for a in AXES)
    core, group, k = net.core, net.group, net.k
    reach = jnp.where(k == 0, 8, k)
    other = lax.rem(group + reach, 16)

    load_q = pltpu.make_async_copy(q_in, q.at[zi, xi, yi, core], lsem.at[0])
    load_q.start()
    load_t = pltpu.make_async_copy(t_in, t, lsem.at[1])
    load_t.start()

    barrier = pltpu.get_barrier_semaphore()

    def greet(device):
        pl.semaphore_signal(barrier, inc=1, device_id=device, device_id_type=MESH)

    for axis in AXES:
        greet(net.neighbour(axis, 1))
        greet(net.neighbour(axis, -1))
    greet(net.sibling())
    for m in range(1, 8):
        greet(member(group, lax.rem(k + m, 8)))
        greet(member(lax.rem(group + 16 - m, 16), jnp.int32(m)))
    greet(member(lax.rem(group + 8, 16), jnp.int32(0)))
    pl.semaphore_wait(barrier, 22)

    load_q.wait()
    gather = [gather_part(net, q, *part) for part in AG_PARTS]
    step_all(gather)
    load_t.wait()

    p[:, :, :, :, pl.ds(B, 8)] = jnp.zeros((4, 4, 4, 2, 8, B), jnp.float32)
    row = lax.broadcasted_iota(jnp.int32, (B, B), 0)
    col = lax.broadcasted_iota(jnp.int32, (B, B), 1)

    def chunk(g, kk):
        return p.at[lax.div(g, 4), lax.rem(g, 4), kk // 2, kk % 2]

    def strip(i):
        left = t[:, pl.ds(pl.multiple_of(i * 256, 256), 256)]
        for j in range(5):
            jj = lax.rem(i + j, 8)
            right = t[:, pl.ds(pl.multiple_of(jj * 256, 256), 256)]
            prod = lax.dot_general(
                left, right, (((0,), (0,)), ((), ())), preferred_element_type=jnp.float32
            )
            for r in range(2):
                for c in range(2):
                    block = prod[r * B : r * B + B, c * B : c * B + B]
                    kk = 2 * j + c - r
                    g = 2 * i + r
                    if 1 <= kk <= 7:
                        chunk(g, kk)[pl.ds(0, B), :] = block
                    elif kk == 8:

                        @pl.when(i < 4)
                        def _(block=block, g=g):
                            chunk(g, 0)[pl.ds(0, B), :] = block

                    elif kk == 0:

                        @pl.when(i < 4)
                        def _(block=block, g=g):
                            chunk(g + 8, 0)[pl.ds(0, B), :] = block

                        @pl.when(i >= 4)
                        def _(block=block, g=g):
                            here = chunk(g, 0)
                            here[pl.ds(0, B), :] = jnp.where(row <= col, here[pl.ds(0, B), :], block)
                            here[pl.ds(B, 1), :] = jnp.sum(
                                jnp.where(row == col, block, 0.0), axis=0, keepdims=True
                            )

    to_sibling = []
    for z in range(4):
        pl.loop(2 * z, 2 * z + 2)(strip)
        to_sibling.append(net.send(p.at[z, :, :, 1 - core], d2d.at[z], net.sibling()))
        step_all(gather)
    for z in range(4):
        to_sibling[z].wait_recv()

        @pl.loop(0, 4)
        def _(i, z=z):
            p[z, i, :, core] += d2d[z, i]

    reduce = [
        reduce_part(net, p, bufs[i], *part) for i, part in enumerate(RS_PARTS)
    ]
    step_all(reduce)
    while gather:
        step_all(gather)

    stores = []
    for z in range(4):

        @pl.loop(0, 4)
        def _(n, z=z):
            rows = pl.ds(pl.multiple_of(n * 256, 256), 256)
            s[pl.ds(512 * z, 512), rows] = lax.dot_general(
                q[z].reshape(512, 2048),
                t[rows, :],
                (((1,), (1,)), ((), ())),
                preferred_element_type=jnp.float32,
            )

        store = pltpu.make_async_copy(
            s.at[pl.ds(512 * z, 512)], s_out.at[pl.ds(512 * z, 512)], lsem.at[2 + z]
        )
        store.start()
        stores.append(store)
        step_all(reduce)
    while reduce:
        step_all(reduce)

    mine = p[zi, xi, yi, core, pl.ds(0, B), :] * scale
    turned = mine.T
    diagonal = p[zi, xi, yi, core, pl.ds(B, 1), :] * scale
    packed = jnp.logical_and(k == 0, group >= 8)
    first = jnp.where(row <= col, mine, turned)
    second = jnp.where(row > col, mine, jnp.where(row < col, turned, jnp.broadcast_to(diagonal, (B, B))))
    x[0] = jnp.where(packed, second, mine).reshape(8, 16, B)
    x[1] = jnp.where(packed, first, turned).reshape(8, 16, B)
    own_slot = jnp.where(packed, group, other)
    other_slot = jnp.where(packed, other, group)
    slots[own_slot] = x[0, k]
    last = []
    for m in range(1, 8):
        to = lax.rem(k + m, 8)
        copy = pltpu.make_async_remote_copy(
            src_ref=x.at[0, to],
            dst_ref=slots.at[own_slot],
            send_sem=xsem.at[0, m],
            recv_sem=xsem.at[1, m],
            device_id=member(group, to),
            device_id_type=MESH,
        )
        copy.start()
        last.append(copy)
    for m in range(8):
        copy = pltpu.make_async_remote_copy(
            src_ref=x.at[1, m],
            dst_ref=slots.at[other_slot],
            send_sem=xsem.at[0, 8 + m],
            recv_sem=xsem.at[1, 8 + k],
            device_id=member(other, jnp.int32(m)),
            device_id_type=MESH,
        )
        copy.start()
        last.append(copy)
    for m in range(1, 16):
        pltpu.make_async_remote_copy(
            src_ref=x.at[0, 0],
            dst_ref=slots.at[0],
            send_sem=xsem.at[0, m],
            recv_sem=xsem.at[1, m],
            device_id=net.sibling(),
            device_id_type=MESH,
        ).wait_recv()
    g_out[...] = slots[...]
    for copy in last + net.sent:
        copy.wait_send()
    for store in stores:
        store.wait()


def local(scale, queries, training):
    n_rows, width = training.shape
    f32, bf16 = jnp.float32, jnp.bfloat16
    scratch = [
        pltpu.VMEM((4, 4, 4, 2, 16, width), bf16),
        pltpu.VMEM((n_rows, width), bf16),
        pltpu.VMEM((4, 4, 4, 2, CH, B), f32),
        pltpu.VMEM((4, 4, 4, CH, B), f32),
        pltpu.VMEM((2048, n_rows), f32),
        pltpu.VMEM((2, 8, 16, B), f32),
        pltpu.VMEM((16, 16, B), f32),
    ]
    for rows, _ in RS_PARTS:
        for shapes in part_buffers(rows):
            scratch += [pltpu.VMEM(shape, f32) for shape in shapes]
    scratch += [
        pltpu.SemaphoreType.DMA((N_SEM,)),
        pltpu.SemaphoreType.DMA((N_SEM,)),
        pltpu.SemaphoreType.DMA((2, 16)),
        pltpu.SemaphoreType.DMA((6,)),
    ]
    scores, slots = pl.pallas_call(
        functools.partial(kernel, scale),
        out_shape=(
            jax.ShapeDtypeStruct((2048, n_rows), f32),
            jax.ShapeDtypeStruct((16, 16, B), f32),
        ),
        in_specs=[pl.BlockSpec(memory_space=pl.ANY)] * 2,
        out_specs=(
            pl.BlockSpec(memory_space=pl.ANY),
            pl.BlockSpec(memory_space=pltpu.VMEM),
        ),
        scratch_shapes=scratch,
        compiler_params=pltpu.CompilerParams(
            collective_id=0, has_side_effects=True, vmem_limit_bytes=60 * 2**20
        ),
        cost_estimate=pl.CostEstimate(
            flops=2 * 2048 * n_rows * 2048 * 2, bytes_accessed=20 * 2**20, transcendentals=0
        ),
    )(queries, training)
    return scores, slots.transpose(1, 0, 2).reshape(16, 2048)


def solution(mesh):
    in_specs = (P(("blk", "grp"), None), P(("blk", "grp"), None))
    out_specs = (P(None, ("blk", "grp")), P(("blk", "grp"), None))
    return jax.shard_map(
        functools.partial(local, 1.0 / 131072),
        mesh=mesh,
        in_specs=in_specs,
        out_specs=out_specs,
        check_vma=False,
    )
```

time: 893 us -> 87.7 us (0.10)
  waiting for transfers between devices: 843 us -> 0 us
  Pallas kernels: 0 us -> 76.9 us
  matrix products: 29.7 us -> 0 us
  between operations: 14 us -> 0.64 us
  local copies, waits for them, and re-layouts: 0 us -> 10 us
    reduce_scatter x1 -> x0, waiting for transfers between devices: 650 us -> none  [local(): lax.psum_scatter(partial_gram, ('blk', 'grp'), scatter_dimension=0, tiled...]
    all_gather x1 -> x0, waiting for transfers between devices: 193 us -> none  [local(): lax.all_gather(queries, ('blk', 'grp'), axis=0, tiled=True)]
    pallas_call x0 -> x1, Pallas kernels: none -> 76.9 us  [local(): pl.pallas_call(functools.partial(kernel, scale), out_shape=(jax.ShapeDtyp...]
    dot_general x2 -> x0, matrix products: 29.7 us -> none  [the longest x1 15.2 us: local(): lax.dot_general(training, training, (((0,), (0,)), ((), ())), preferred_e...]
  transfers between devices with their start and end apart: 2 -> 0, of which waited for: 2 -> 0; matrix products, arithmetic and copies ran while one was open for 3% -> 0% of each run, Pallas kernels for 0% -> 0%
where the time goes in v1:
time: 87.7 us; the launch traced here: 87.6 us
  Pallas kernels  76.9 us (88%)
  local copies, waits for them, and re-layouts  10 us (11%)
    pallas_call x1, Pallas kernels, local(): pl.pallas_call(functools.partial(kernel, scale), out_shape=(jax.ShapeDtyp...  76.9 us
    unnamed x1, local copies, waits for them, and re-layouts  8.44 us

profile of v1, /device:TPU:1, one launch (start us, length us, event | category | flops | bytes accessed | tf_op | source)
XLA Modules:
  0.0 87.6 jit_solution(9021424251930459361)
XLA Ops:
  0.6 76.9 %shard_map.41 = (f32[2048,1024]{1,0:T(8,128)}, f32[16,16,128]{2,1,0:T(8,128)}) custom-call(bf16[16,2048]{1,0:T(8,128)(2,1)} %refs_0_.1, bf16[1024,2048]{1,0:T(8,128)(2,1)} %refs_1_.1), custom_call_target="tpu_custom_call" | custom-call | flops 17179869184 | bytes 20971520 | tf_op jit(solution)/shard_map/pallas_call | solution.py:377
  77.5 1.6 %copy_bitcast_fusion = f32[16,2048]{1,0:T(8,128)} fusion(f32[16,16,128]{2,1,0:T(8,128)} %get-tuple-element.5), kind=kLoop, calls=%fused_computation | loop fusion | bytes 262144 | tf_op jit(solution)/shard_map/reshape | solution.py:396
  79.1 8.4 %copy.8 = f32[2048,1024]{1,0:T(8,128)} copy(f32[2048,1024]{1,0:T(8,128)} %get-tuple-element.8) | data formatting | bytes 16777216
